TPU v7x, 32 devices: a whole 2x2x4 slice. The times are simulated.
32 devices in a mesh: tile: 8 (over z, x), lev: 4 (over y, core).
Axes of the slice: x: 2, y: 2, z: 4, core: 2. Of those that a mesh axis runs over, the one named last changes fastest.
Arguments:
- fields: float32 [2, 60, 1024, 128], P(None, 'lev', 'tile'), may hold values from -6 to 6
- wind_x: float32 [60, 1024, 128], P('lev', 'tile'), may hold values from -0.8 to 0.8
- wind_y: float32 [60, 1024, 128], P('lev', 'tile'), may hold values from -0.8 to 0.8
- diffusivity: float32 [60, 1024, 128], P('lev', 'tile'), may hold values from 0.02 to 0.3
- surface: float32 [8, 131072], P(None, ('tile', 'lev')), may hold values from -6 to 6
- cloud_list: int32 [131072], P(('tile', 'lev')), may hold values from -1 to 4095, as said below
- input_weight: bfloat16 [128, 512], replicated, may hold values from -0.5 to 0.5
- hidden_weight: bfloat16 [5, 512, 512], replicated, may hold values from -0.25 to 0.25
- output_weight: bfloat16 [512, 128], replicated, may hold values from -0.25 to 0.25
- clear_weight: bfloat16 [128, 128], replicated, may hold values from -0.5 to 0.5
Outputs:
- fields_out: float32 [2, 60, 131072], P(None, None, ('tile', 'lev'))
- surface_out: float32 [8, 131072], P(None, ('tile', 'lev'))
Inputs may be any that keep to these rules, and one draw needn't show every extreme that they name: `cloud_list`: block d of 4096 entries belongs to the device of tile index d // 4 and lev index d % 4, whose columns are d * 4096 onward. Each block lists distinct local indices of cloudy columns in any order, then -1 to its end. Over the 8 blocks of one lev index, the numbers ceil(cloudy count / 512) sum to more than (3) * 8 and at most 32.
All inputs are finite; a program needn't handle non-finite values.
Results may differ from a plain program's by a relative error of at most 0.0055.
Values may be sent and summed in bfloat16 or wider, within the bound.
A program may use at most 128 MiB of HBM per device.

v0:
```python
import functools

import numpy as np
import jax
import jax.numpy as jnp
from jax import lax
from jax.experimental import pallas as pl
from jax.experimental.pallas import tpu as pltpu
from jax.sharding import PartitionSpec as P

F32 = jnp.float32
BF16 = jnp.bfloat16
ROWS = 8
VMEM_LIMIT = 56 * 1024 * 1024


def advect_kernel(
    tiles, levs, lb, lp, nx, ny,
    f_hbm, wx_hbm, wy_hbm, d_hbm, out_ref,
    fv, wv, padded, coef, edge_out, edge_in, outbox,
    load_sem, halo_send, halo_recv, part_send, part_recv,
):
    tile = lax.axis_index("tile")
    me = lax.axis_index("lev")
    right = lax.rem(tile + 1, tiles)
    left = lax.rem(tile + tiles - 1, tiles)
    mine = nx // levs
    steps = mine // ROWS
    group = 2 * lp

    loads = [pltpu.make_async_copy(f_hbm, fv.at[pl.ds(0, 2 * lb * nx)], load_sem.at[0])]
    for i, ref in enumerate((wx_hbm, wy_hbm, d_hbm)):
        loads.append(
            pltpu.make_async_copy(ref, wv.at[pl.ds(i * lp * nx, lb * nx)], load_sem.at[i + 1])
        )
    for copy in loads:
        copy.start()

    barrier = pltpu.get_barrier_semaphore()
    for near in (left, right):
        pl.semaphore_signal(
            barrier, inc=1, device_id={"tile": near}, device_id_type=pl.DeviceIdType.MESH
        )
    for o in range(1, levs):
        pl.semaphore_signal(
            barrier, inc=1, device_id={"lev": lax.rem(me + o, levs)},
            device_id_type=pl.DeviceIdType.MESH,
        )

    extra = lp - lb
    if extra:
        fv[pl.ds(2 * lb * nx, extra * nx), :] = jnp.zeros((extra * nx, ny), F32)
        for i in range(3):
            wv[pl.ds((i * lp + lb) * nx, extra * nx), :] = jnp.zeros((extra * nx, ny), F32)

    lane = lax.broadcasted_iota(jnp.int32, (lp, ny), 1)
    north_ok = lane < ny - 1
    south_ok = lane > 0

    def level_rows(ref, first, x):
        parts = [ref[pl.ds((first + 8 * h) * nx + x, 8, stride=nx), :] for h in range(lp // 8)]
        return jnp.concatenate(parts, axis=0)

    def convert(x):
        for v in range(2):
            padded[x + 3, v * lp : (v + 1) * lp, :] = level_rows(fv, v * lb, x)

    def set_coef(row, wx, wy, d):
        wx = 0.5 * wx
        wy = 0.5 * wy
        coef[row, 0] = d - wx
        coef[row, 1] = d + wx
        coef[row, 2] = jnp.where(north_ok, d - wy, 0.0)
        coef[row, 3] = jnp.where(south_ok, d + wy, 0.0)
        coef[row, 4] = 4.0 * d

    for copy in loads:
        copy.wait()
    for x in (0, 1, 2, nx - 3, nx - 2, nx - 1):
        convert(x)
    for side, first in ((0, 0), (1, nx - 2)):
        for r in range(2):
            for i in range(3):
                edge_out[side, r * 3 + i] = level_rows(wv, i * lp, first + r)

    pl.semaphore_wait(barrier, 2 + levs - 1)

    def halo_copy(src, dst, index, near):
        return pltpu.make_async_remote_copy(
            src_ref=src, dst_ref=dst, send_sem=halo_send.at[index], recv_sem=halo_recv.at[index],
            device_id={"tile": near}, device_id_type=pl.DeviceIdType.MESH,
        )

    halos = [
        halo_copy(padded.at[pl.ds(nx, 3)], padded.at[pl.ds(0, 3)], 0, right),
        halo_copy(padded.at[pl.ds(3, 3)], padded.at[pl.ds(nx + 3, 3)], 1, left),
        halo_copy(edge_out.at[1], edge_in.at[0], 2, right),
        halo_copy(edge_out.at[0], edge_in.at[1], 3, left),
    ]
    for copy in halos:
        copy.start()

    @pl.loop(3, nx - 3)
    def _(x):
        convert(x)

    @pl.loop(0, nx)
    def _(x):
        set_coef(x + 2, *(level_rows(wv, i * lp, x) for i in range(3)))

    def rate(c, e, w, row):
        north = pltpu.roll(c, ny - 1, axis=1)
        south = pltpu.roll(c, 1, axis=1)
        return (
            coef[row, 0] * e + coef[row, 1] * w + coef[row, 2] * north + coef[row, 3] * south
            - coef[row, 4] * c
        )

    def section(x0, save):
        for v in range(2):
            lo, hi = v * lp, (v + 1) * lp
            f = [padded[x0 + i, lo:hi, :] for i in range(2)]
            one = []
            two = []
            for r in range(ROWS + 4):
                f.append(padded[x0 + r + 2, lo:hi, :])
                one.append(f[r + 1] + rate(f[r + 1], f[r + 2], f[r], x0 + r) * (1.0 / 3.0))
                if r >= 2:
                    two.append(
                        f[r] + 0.5 * rate(one[r - 1], one[r], one[r - 2], x0 + r - 1)
                    )
                if r >= 4:
                    done = f[r - 1] + rate(two[r - 3], two[r - 2], two[r - 4], x0 + r - 2)
                    save(r - 4, lo, done.astype(BF16))

    def part_copy(k, o, source):
        return pltpu.make_async_remote_copy(
            src_ref=outbox.at[o - 1, pl.ds(k * ROWS, ROWS)],
            dst_ref=out_ref.at[pl.ds(k * ROWS, ROWS), pl.ds(pl.multiple_of(source * group, group), group)],
            send_sem=part_send.at[k, o - 1],
            recv_sem=part_recv.at[k, o - 1],
            device_id={"lev": lax.rem(me + o, levs)},
            device_id_type=pl.DeviceIdType.MESH,
        )

    def step(k):
        @pl.loop(1, levs)
        def _(o):
            def save(r, lo, value):
                outbox[o - 1, k * ROWS + r, lo : lo + lp, :] = value

            section(lax.rem(me + o, levs) * mine + k * ROWS, save)
            part_copy(k, o, me).start()

    def own(k):
        base = pl.multiple_of(me * group, group)

        def save(r, lo, value):
            out_ref[k * ROWS + r, pl.ds(base + lo, lp), :] = value

        section(me * mine + k * ROWS, save)

    @pl.loop(1, steps - 1)
    def _(k):
        step(k)

    for copy in halos:
        copy.wait()
    for side, first in ((0, 0), (1, nx + 2)):
        for r in range(2):
            set_coef(first + r, *(edge_in[side, r * 3 + i] for i in range(3)))

    @pl.loop(0, 2)
    def _(i):
        step(i * (steps - 1))

    @pl.loop(0, steps)
    def _(k):
        own(k)

    @pl.loop(0, steps)
    def _(k):
        @pl.loop(1, levs)
        def _(o):
            part_copy(k, o, me).wait_send()
            part_copy(k, o, lax.rem(me + levs - o, levs)).wait_recv()


def nt(a, b):
    return lax.dot_general(a, b, (((1,), (1,)), ((), ())), preferred_element_type=F32)


def silu(v):
    h = 0.5 * v
    return h * jnp.tanh(h) + h


def physics_kernel(
    rows, lanes, groups, levels, level_pad, layers,
    feat_ref, surf_ref, cloud_ref, pin_ref, pout_ref, move_ref, iw_ref, hw_ref, ow_ref, cw_ref,
    fields_ref, surface_ref,
    mask, iw, ow, cw,
):
    step = pl.program_id(0)

    @pl.when(step == 0)
    def _():
        listed = cloud_ref[...]
        count = listed.shape[1]
        high = lax.broadcasted_iota(jnp.int32, (mask.shape[0], count), 0)
        low = lax.broadcasted_iota(jnp.int32, (lanes, count), 0)
        top = jnp.right_shift(listed, int(lanes).bit_length() - 1)
        hot_high = jnp.where(high == top, 1.0, 0.0).astype(BF16)
        hot_low = jnp.where(low == jnp.bitwise_and(listed, lanes - 1), 1.0, 0.0).astype(BF16)
        mask[...] = nt(hot_high, hot_low)
        iw[...] = jnp.dot(pin_ref[...], iw_ref[...], preferred_element_type=F32).astype(BF16)
        ow[...] = nt(pout_ref[...], ow_ref[...]).astype(BF16)
        turned = nt(pout_ref[...], cw_ref[...]).astype(BF16)
        cw[: turned.shape[0], :] = nt(turned, pin_ref[...]).astype(BF16)
        cw[turned.shape[0] :, :] = move_ref[...]

    surf = surf_ref[...]
    surf16 = surf.astype(BF16)
    tail = jnp.concatenate([surf16, jnp.zeros_like(surf16)], axis=0)
    feat = jnp.concatenate([feat_ref[r] for r in range(rows)], axis=1)
    feat = jnp.concatenate([feat, tail], axis=0)

    half = rows * lanes // 2
    streams = []
    for s in range(2):
        piece = feat[:, s * half : (s + 1) * half]
        streams.append(
            silu(lax.dot_general(piece, iw[...], (((0,), (0,)), ((), ())), preferred_element_type=F32))
        )
    for layer in range(layers):
        for s in range(2):
            streams[s] = streams[s] + silu(
                jnp.dot(streams[s].astype(BF16), hw_ref[layer], preferred_element_type=F32)
            )
    both = jnp.dot(cw[...], feat, preferred_element_type=F32)
    out_rows = ow.shape[0]
    for s in range(2):
        physics = nt(ow[...], streams[s].astype(BF16)).astype(BF16).astype(F32)
        keep = jnp.concatenate(
            [mask[pl.ds(step * rows + s * (rows // 2) + r, 1), :] for r in range(rows // 2)], axis=1
        )
        at = slice(s * half, (s + 1) * half)
        tend = both[:out_rows, at] + jnp.where(keep > 0.5, physics, 0.0)
        tend = tend.astype(BF16).astype(F32)
        for v in range(2):
            first = v * level_pad
            fields_ref[v, :, at] = (
                both[out_rows + first : out_rows + first + levels, at]
                + tend[first : first + levels]
            )
        surface_ref[:, at] = surf[:, at] + tend[2 * level_pad : 2 * level_pad + surf.shape[0]]


def orders(levs, lb, lp, levels, level_pad, surf, features):
    size_in = levs * 2 * lp + 2 * surf
    size_out = 2 * level_pad + 2 * surf
    pin = np.zeros((size_in, features), np.float32)
    pout = np.zeros((size_out, features), np.float32)
    for v in range(2):
        for level in range(levels):
            j, l = divmod(level, lb)
            pin[j * 2 * lp + v * lp + l, v * levels + level] = 1.0
            pout[v * level_pad + level, v * levels + level] = 1.0
    for s in range(surf):
        pin[levs * 2 * lp + s, 2 * levels + s] = 1.0
        pout[2 * level_pad + s, 2 * levels + s] = 1.0
    return pin, pout, pout @ pin.T


def local(
    tiles, levs,
    fields, wind_x, wind_y, diffusivity, surface, cloud_list,
    input_weight, hidden_weight, output_weight, clear_weight,
):
    _, lb, nx, ny = fields.shape
    lp = -(-lb // 8) * 8
    levels = lb * levs
    level_pad = -(-levels // 8) * 8
    mine = nx // levs
    group = 2 * lp
    any_spec = pl.BlockSpec(memory_space=pl.ANY)
    vmem_spec = pl.BlockSpec(memory_space=pltpu.VMEM)
    parts = mine // ROWS
    feats = pl.pallas_call(
        functools.partial(advect_kernel, tiles, levs, lb, lp, nx, ny),
        out_shape=jax.ShapeDtypeStruct((mine, levs * group, ny), BF16),
        in_specs=[any_spec] * 4,
        out_specs=vmem_spec,
        scratch_shapes=[
            pltpu.VMEM(((2 * lb + lp - lb) * nx, ny), F32),
            pltpu.VMEM((3 * lp * nx, ny), F32),
            pltpu.VMEM((nx + 6, group, ny), F32),
            pltpu.VMEM((nx + 4, 5, lp, ny), F32),
            pltpu.VMEM((2, 6, lp, ny), F32),
            pltpu.VMEM((2, 6, lp, ny), F32),
            pltpu.VMEM((levs - 1, mine, group, ny), BF16),
            pltpu.SemaphoreType.DMA((4,)),
            pltpu.SemaphoreType.DMA((4,)),
            pltpu.SemaphoreType.DMA((4,)),
            pltpu.SemaphoreType.DMA((parts, levs - 1)),
            pltpu.SemaphoreType.DMA((parts, levs - 1)),
        ],
        compiler_params=pltpu.CompilerParams(
            collective_id=0, has_side_effects=True, vmem_limit_bytes=VMEM_LIMIT
        ),
        name="advect",
    )(
        fields.reshape(2 * lb * nx, ny),
        wind_x.reshape(lb * nx, ny),
        wind_y.reshape(lb * nx, ny),
        diffusivity.reshape(lb * nx, ny),
    )

    surf, cols = surface.shape
    features, hid = input_weight.shape
    layers = hidden_weight.shape[0]
    pin, pout, move = (
        jnp.asarray(m, BF16) for m in orders(levs, lb, lp, levels, level_pad, surf, features)
    )
    size_in, size_out = pin.shape[0], pout.shape[0]
    rows = 8
    wide = rows * ny
    return pl.pallas_call(
        functools.partial(physics_kernel, rows, ny, levs, levels, level_pad, layers),
        grid=(mine // rows,),
        out_shape=(
            jax.ShapeDtypeStruct((2, levels, cols), F32),
            jax.ShapeDtypeStruct((surf, cols), F32),
        ),
        in_specs=[
            pl.BlockSpec((rows, levs * group, ny), lambda i: (i, 0, 0)),
            pl.BlockSpec((surf, wide), lambda i: (0, i)),
        ] + [vmem_spec] * 8,
        out_specs=(
            pl.BlockSpec((2, levels, wide), lambda i: (0, 0, i)),
            pl.BlockSpec((surf, wide), lambda i: (0, i)),
        ),
        scratch_shapes=[
            pltpu.VMEM((mine, ny), F32),
            pltpu.VMEM((size_in, hid), BF16),
            pltpu.VMEM((size_out, hid), BF16),
            pltpu.VMEM((2 * size_out, size_in), BF16),
        ],
        compiler_params=pltpu.CompilerParams(vmem_limit_bytes=VMEM_LIMIT),
        name="physics",
    )(
        feats, surface, cloud_list.reshape(1, -1), pin, pout, move,
        input_weight, hidden_weight, output_weight, clear_weight,
    )


def solution(mesh):
    return jax.shard_map(
        functools.partial(local, mesh.shape["tile"], mesh.shape["lev"]),
        mesh=mesh,
        in_specs=(
            P(None, "lev", "tile", None),
            P("lev", "tile", None),
            P("lev", "tile", None),
            P("lev", "tile", None),
            P(None, ("tile", "lev")),
            P(("tile", "lev")),
            P(),
            P(),
            P(),
            P(),
        ),
        out_specs=(P(None, None, ("tile", "lev")), P(None, ("tile", "lev"))),
        check_vma=False,
    )
```

profile of v0, /device:TPU:0, one launch (start us, length us, event | category | flops | bytes accessed | tf_op | source)
XLA Modules:
  0.0 52.0 jit_solution(17329924031769018618)
XLA Ops:
  0.6 26.8 %advect.1.feat_ref = bf16[32,128,128]{2,1,0:T(8,128)(2,1)} custom-call(f32[3840,128]{1,0:T(8,128)} %bitcast.5, f32[1920,128]{1,0:T(8,128)} %bitcast.6, f32[1920,128]{1,0:T(8,128)} %bitcast.7, f32[1920,128]{1,0:T(8,128)} %bitcast.8), custom_call_target="tpu_custom_call" | custom-call | tf_op jit(solution)/shard_map/advect/pallas_call | solution.py:289
  27.4 20.2 %physics.1 = (f32[2,60,4096]{2,1,0:T(8,128)}, f32[8,4096]{1,0:T(8,128)}) custom-call(bf16[32,128,128]{2,1,0:T(8,128)(2,1)} %advect.1.feat_ref, f32[8,4096]{1,0:T(8,128)} %surf_ref.1, s32[1,4096]{1,0:T(1,128)} %bitcast.9, bf16[144,128]{1,0:T(8,128)(2,1)} %constant.6.clone.pin_ref, bf16[144,128]{1,0:T(8,128)(2,1)} %constant.7.clone.pout_ref, ...), custom_call_target="tpu_custom_call" | custom-call | tf_op jit(solution)/shard_map/physics/pallas_call | solution.py:328
  47.6 4.4 %copy.15 = f32[2,60,4096]{2,0,1:T(2,128)} copy(f32[2,60,4096]{2,1,0:T(8,128)} %get-tuple-element.2) | data formatting | bytes 3932160 | tf_op jit(solution)/shard_map/physics/pallas_call | solution.py:328
where the time goes:
time: 52.2 us; the launch traced here: 52 us
  Pallas kernels  47 us (90%)
  local copies, waits for them, and re-layouts  4.38 us (8%)
  between operations  0.64 us (1%)
    pallas_call x1, Pallas kernels, local(): pl.pallas_call(functools.partial(advect_kernel, tiles, levs, lb, lp, nx,...  26.8 us
    pallas_call x1, Pallas kernels, local(): pl.pallas_call(functools.partial(physics_kernel, rows, ny, levs, levels,...  20.2 us
    pallas_call x1, local copies, waits for them, and re-layouts, local(): pl.pallas_call(functools.partial(physics_kernel, rows, ny, levs, levels,...  4.38 us

commit v1 on v0

--- a/solution.py
+++ b/solution.py
@@ -11,15 +11,19 @@
 F32 = jnp.float32
 BF16 = jnp.bfloat16
 ROWS = 8
-VMEM_LIMIT = 56 * 1024 * 1024
+ADVECT_VMEM = 58 * 1024 * 1024
+PHYSICS_VMEM = 58 * 1024 * 1024
 
 
 def advect_kernel(
     tiles, levs, lb, lp, nx, ny,
-    f_hbm, wx_hbm, wy_hbm, d_hbm, out_ref,
-    fv, wv, padded, coef, edge_out, edge_in, outbox,
-    load_sem, halo_send, halo_recv, part_send, part_recv,
+    f_hbm, wx_hbm, wy_hbm, d_hbm, *refs,
 ):
+    small_hbm, refs = refs[:7], refs[7:]
+    out_ref, mask, iw, ow, cw = refs[:5]
+    small, refs = refs[5:12], refs[12:]
+    fv, wv, padded, coef, edge_out, edge_in, outbox, load_sem, small_sem = refs[:9]
+    halo_send, halo_recv, part_send, part_recv = refs[9:]
     tile = lax.axis_index("tile")
     me = lax.axis_index("lev")
     right = lax.rem(tile + 1, tiles)
@@ -33,7 +37,11 @@
         loads.append(
             pltpu.make_async_copy(ref, wv.at[pl.ds(i * lp * nx, lb * nx)], load_sem.at[i + 1])
         )
-    for copy in loads:
+    extras = [
+        pltpu.make_async_copy(src, dst, small_sem.at[i])
+        for i, (src, dst) in enumerate(zip(small_hbm, small))
+    ]
+    for copy in loads + extras:
         copy.start()
 
     barrier = pltpu.get_barrier_semaphore()
@@ -100,13 +108,16 @@
     for copy in halos:
         copy.start()
 
-    @pl.loop(3, nx - 3)
-    def _(x):
-        convert(x)
-
-    @pl.loop(0, nx)
-    def _(x):
-        set_coef(x + 2, *(level_rows(wv, i * lp, x) for i in range(3)))
+    @pl.loop(0, nx // 8)
+    def _(b):
+        for r in range(8):
+            x = b * 8 + r
+            set_coef(x + 2, *(level_rows(wv, i * lp, x) for i in range(3)))
+
+    @pl.loop(0, (nx - 6) // 2, unroll=4)
+    def _(b):
+        for r in range(2):
+            convert(3 + b * 2 + r)
 
     def rate(c, e, w, row):
         north = pltpu.roll(c, ny - 1, axis=1)
@@ -133,24 +144,30 @@
                     done = f[r - 1] + rate(two[r - 3], two[r - 2], two[r - 4], x0 + r - 2)
                     save(r - 4, lo, done.astype(BF16))
 
+    pair = 2 if levs % 2 == 0 else 1
+    chips = levs // pair
+    high, low = me // pair, lax.rem(me, pair)
+
+    def peer(o, sign):
+        far = lax.rem(high + (o // pair if sign > 0 else chips - o // pair), chips)
+        return far * pair + lax.rem(low + (o % pair if sign > 0 else pair - o % pair), pair)
+
     def part_copy(k, o, source):
         return pltpu.make_async_remote_copy(
             src_ref=outbox.at[o - 1, pl.ds(k * ROWS, ROWS)],
             dst_ref=out_ref.at[pl.ds(k * ROWS, ROWS), pl.ds(pl.multiple_of(source * group, group), group)],
             send_sem=part_send.at[k, o - 1],
             recv_sem=part_recv.at[k, o - 1],
-            device_id={"lev": lax.rem(me + o, levs)},
+            device_id={"lev": peer(o, 1)},
             device_id_type=pl.DeviceIdType.MESH,
         )
 
-    def step(k):
-        @pl.loop(1, levs)
-        def _(o):
-            def save(r, lo, value):
-                outbox[o - 1, k * ROWS + r, lo : lo + lp, :] = value
-
-            section(lax.rem(me + o, levs) * mine + k * ROWS, save)
-            part_copy(k, o, me).start()
+    def step(k, o):
+        def save(r, lo, value):
+            outbox[o - 1, k * ROWS + r, lo : lo + lp, :] = value
+
+        section(peer(o, 1) * mine + k * ROWS, save)
+        part_copy(k, o, me).start()
 
     def own(k):
         base = pl.multiple_of(me * group, group)
@@ -162,7 +179,9 @@
 
     @pl.loop(1, steps - 1)
     def _(k):
-        step(k)
+        @pl.loop(pair, levs)
+        def _(o):
+            step(k, o)
 
     for copy in halos:
         copy.wait()
@@ -172,22 +191,51 @@
 
     @pl.loop(0, 2)
     def _(i):
-        step(i * (steps - 1))
+        @pl.loop(pair, levs)
+        def _(o):
+            step(i * (steps - 1), o)
+
+    @pl.loop(0, steps)
+    def _(k):
+        @pl.loop(1, pair)
+        def _(o):
+            step(k, o)
 
     @pl.loop(0, steps)
     def _(k):
         own(k)
+
+    for copy in extras:
+        copy.wait()
+    prepare(*small, mask, iw, ow, cw)
 
     @pl.loop(0, steps)
     def _(k):
         @pl.loop(1, levs)
         def _(o):
             part_copy(k, o, me).wait_send()
-            part_copy(k, o, lax.rem(me + levs - o, levs)).wait_recv()
+            part_copy(k, o, peer(o, -1)).wait_recv()
 
 
 def nt(a, b):
     return lax.dot_general(a, b, (((1,), (1,)), ((), ())), preferred_element_type=F32)
+
+
+def prepare(cloud_ref, pin_ref, pout_ref, move_ref, iw_ref, ow_ref, cw_ref, mask, iw, ow, cw):
+    listed = cloud_ref[...]
+    count = listed.shape[1]
+    lanes = mask.shape[1]
+    high = lax.broadcasted_iota(jnp.int32, (mask.shape[0], count), 0)
+    low = lax.broadcasted_iota(jnp.int32, (lanes, count), 0)
+    shift = lanes.bit_length() - 1
+    hot_high = jnp.where(high == jnp.right_shift(listed, shift), 1.0, 0.0).astype(BF16)
+    hot_low = jnp.where(low == jnp.bitwise_and(listed, lanes - 1), 1.0, 0.0).astype(BF16)
+    mask[...] = nt(hot_high, hot_low)
+    iw[...] = jnp.dot(pin_ref[...], iw_ref[...], preferred_element_type=F32).astype(BF16)
+    ow[...] = nt(pout_ref[...], ow_ref[...]).astype(BF16)
+    turned = nt(pout_ref[...], cw_ref[...]).astype(BF16)
+    cw[: turned.shape[0], :] = nt(turned, pin_ref[...]).astype(BF16)
+    cw[turned.shape[0] :, :] = move_ref[...]
 
 
 def silu(v):
@@ -196,29 +244,10 @@
 
 
 def physics_kernel(
-    rows, lanes, groups, levels, level_pad, layers,
-    feat_ref, surf_ref, cloud_ref, pin_ref, pout_ref, move_ref, iw_ref, hw_ref, ow_ref, cw_ref,
-    fields_ref, surface_ref,
-    mask, iw, ow, cw,
+    rows, lanes, levels, level_pad, layers,
+    feat_ref, surf_ref, mask, iw, hw_ref, ow, cw, fields_ref, surface_ref,
 ):
     step = pl.program_id(0)
-
-    @pl.when(step == 0)
-    def _():
-        listed = cloud_ref[...]
-        count = listed.shape[1]
-        high = lax.broadcasted_iota(jnp.int32, (mask.shape[0], count), 0)
-        low = lax.broadcasted_iota(jnp.int32, (lanes, count), 0)
-        top = jnp.right_shift(listed, int(lanes).bit_length() - 1)
-        hot_high = jnp.where(high == top, 1.0, 0.0).astype(BF16)
-        hot_low = jnp.where(low == jnp.bitwise_and(listed, lanes - 1), 1.0, 0.0).astype(BF16)
-        mask[...] = nt(hot_high, hot_low)
-        iw[...] = jnp.dot(pin_ref[...], iw_ref[...], preferred_element_type=F32).astype(BF16)
-        ow[...] = nt(pout_ref[...], ow_ref[...]).astype(BF16)
-        turned = nt(pout_ref[...], cw_ref[...]).astype(BF16)
-        cw[: turned.shape[0], :] = nt(turned, pin_ref[...]).astype(BF16)
-        cw[turned.shape[0] :, :] = move_ref[...]
-
     surf = surf_ref[...]
     surf16 = surf.astype(BF16)
     tail = jnp.concatenate([surf16, jnp.zeros_like(surf16)], axis=0)
@@ -232,13 +261,22 @@
         streams.append(
             silu(lax.dot_general(piece, iw[...], (((0,), (0,)), ((), ())), preferred_element_type=F32))
         )
+    hid = hw_ref.shape[2]
+    cuts = [slice(c, min(c + 256, hid)) for c in range(0, hid, 256)]
     for layer in range(layers):
         for s in range(2):
-            streams[s] = streams[s] + silu(
-                jnp.dot(streams[s].astype(BF16), hw_ref[layer], preferred_element_type=F32)
+            operand = streams[s].astype(BF16)
+            streams[s] = jnp.concatenate(
+                [
+                    streams[s][:, cut]
+                    + silu(jnp.dot(operand, hw_ref[layer, :, cut], preferred_element_type=F32))
+                    for cut in cuts
+                ],
+                axis=1,
             )
     both = jnp.dot(cw[...], feat, preferred_element_type=F32)
     out_rows = ow.shape[0]
+    flat = fields_ref.reshape(levels * 2 * rows, lanes)
     for s in range(2):
         physics = nt(ow[...], streams[s].astype(BF16)).astype(BF16).astype(F32)
         keep = jnp.concatenate(
@@ -249,10 +287,17 @@
         tend = tend.astype(BF16).astype(F32)
         for v in range(2):
             first = v * level_pad
-            fields_ref[v, :, at] = (
-                both[out_rows + first : out_rows + first + levels, at]
-                + tend[first : first + levels]
+            total = (
+                both[out_rows + first : out_rows + first + level_pad, at]
+                + tend[first : first + level_pad]
             )
+            for r in range(rows // 2):
+                place = 2 * (s * (rows // 2) + r) + v
+                for l in range(0, levels, 8):
+                    n = min(8, levels - l)
+                    flat[pl.ds(l * 2 * rows + place, n, stride=2 * rows), :] = (
+                        total[l : l + n, r * lanes : (r + 1) * lanes]
+                    )
         surface_ref[:, at] = surf[:, at] + tend[2 * level_pad : 2 * level_pad + surf.shape[0]]
 
 
@@ -286,12 +331,26 @@
     any_spec = pl.BlockSpec(memory_space=pl.ANY)
     vmem_spec = pl.BlockSpec(memory_space=pltpu.VMEM)
     parts = mine // ROWS
-    feats = pl.pallas_call(
+    surf, cols = surface.shape
+    features, hid = input_weight.shape
+    layers = hidden_weight.shape[0]
+    orderings = [
+        jnp.asarray(m, BF16) for m in orders(levs, lb, lp, levels, level_pad, surf, features)
+    ]
+    size_out, size_in = orderings[2].shape
+    small = [cloud_list.reshape(1, -1), *orderings, input_weight, output_weight, clear_weight]
+    feats, mask, iw, ow, cw = pl.pallas_call(
         functools.partial(advect_kernel, tiles, levs, lb, lp, nx, ny),
-        out_shape=jax.ShapeDtypeStruct((mine, levs * group, ny), BF16),
-        in_specs=[any_spec] * 4,
-        out_specs=vmem_spec,
-        scratch_shapes=[
+        out_shape=(
+            jax.ShapeDtypeStruct((mine, levs * group, ny), BF16),
+            jax.ShapeDtypeStruct((mine, ny), F32),
+            jax.ShapeDtypeStruct((size_in, hid), BF16),
+            jax.ShapeDtypeStruct((size_out, hid), BF16),
+            jax.ShapeDtypeStruct((2 * size_out, size_in), BF16),
+        ),
+        in_specs=[any_spec] * (4 + len(small)),
+        out_specs=(vmem_spec,) * 5,
+        scratch_shapes=[pltpu.VMEM(a.shape, a.dtype) for a in small] + [
             pltpu.VMEM(((2 * lb + lp - lb) * nx, ny), F32),
             pltpu.VMEM((3 * lp * nx, ny), F32),
             pltpu.VMEM((nx + 6, group, ny), F32),
@@ -300,13 +359,14 @@
             pltpu.VMEM((2, 6, lp, ny), F32),
             pltpu.VMEM((levs - 1, mine, group, ny), BF16),
             pltpu.SemaphoreType.DMA((4,)),
+            pltpu.SemaphoreType.DMA((len(small),)),
             pltpu.SemaphoreType.DMA((4,)),
             pltpu.SemaphoreType.DMA((4,)),
             pltpu.SemaphoreType.DMA((parts, levs - 1)),
             pltpu.SemaphoreType.DMA((parts, levs - 1)),
         ],
         compiler_params=pltpu.CompilerParams(
-            collective_id=0, has_side_effects=True, vmem_limit_bytes=VMEM_LIMIT
+            collective_id=0, has_side_effects=True, vmem_limit_bytes=ADVECT_VMEM
         ),
         name="advect",
     )(
@@ -314,44 +374,31 @@
         wind_x.reshape(lb * nx, ny),
         wind_y.reshape(lb * nx, ny),
         diffusivity.reshape(lb * nx, ny),
+        *small,
     )
 
-    surf, cols = surface.shape
-    features, hid = input_weight.shape
-    layers = hidden_weight.shape[0]
-    pin, pout, move = (
-        jnp.asarray(m, BF16) for m in orders(levs, lb, lp, levels, level_pad, surf, features)
-    )
-    size_in, size_out = pin.shape[0], pout.shape[0]
     rows = 8
     wide = rows * ny
-    return pl.pallas_call(
-        functools.partial(physics_kernel, rows, ny, levs, levels, level_pad, layers),
+    fields_out, surface_out = pl.pallas_call(
+        functools.partial(physics_kernel, rows, ny, levels, level_pad, layers),
         grid=(mine // rows,),
         out_shape=(
-            jax.ShapeDtypeStruct((2, levels, cols), F32),
+            jax.ShapeDtypeStruct((levels, mine * 2, ny), F32),
             jax.ShapeDtypeStruct((surf, cols), F32),
         ),
         in_specs=[
             pl.BlockSpec((rows, levs * group, ny), lambda i: (i, 0, 0)),
             pl.BlockSpec((surf, wide), lambda i: (0, i)),
-        ] + [vmem_spec] * 8,
+        ] + [vmem_spec] * 5,
         out_specs=(
-            pl.BlockSpec((2, levels, wide), lambda i: (0, 0, i)),
+            pl.BlockSpec((levels, 2 * rows, ny), lambda i: (0, i, 0)),
             pl.BlockSpec((surf, wide), lambda i: (0, i)),
         ),
-        scratch_shapes=[
-            pltpu.VMEM((mine, ny), F32),
-            pltpu.VMEM((size_in, hid), BF16),
-            pltpu.VMEM((size_out, hid), BF16),
-            pltpu.VMEM((2 * size_out, size_in), BF16),
-        ],
-        compiler_params=pltpu.CompilerParams(vmem_limit_bytes=VMEM_LIMIT),
+        compiler_params=pltpu.CompilerParams(vmem_limit_bytes=PHYSICS_VMEM),
         name="physics",
-    )(
-        feats, surface, cloud_list.reshape(1, -1), pin, pout, move,
-        input_weight, hidden_weight, output_weight, clear_weight,
-    )
+    )(feats, surface, mask, iw, hidden_weight, ow, cw)
+    fields_out = fields_out.reshape(levels, mine, 2, ny).transpose(2, 0, 1, 3)
+    return fields_out.reshape(2, levels, cols), surface_out
 
 
 def solution(mesh):

time: 52.2 us -> 44.7 us (0.86)
  local copies, waits for them, and re-layouts: 4.38 us -> 0 us
  Pallas kernels: 47 us -> 43.8 us
    pallas_call x1 -> x0, local copies, waits for them, and re-layouts: 4.38 us -> none  [local(): pl.pallas_call(functools.partial(physics_kernel, rows, ny, levs, levels,...]
    pallas_call x1, Pallas kernels: 26.8 us -> 24.1 us  [local(): pl.pallas_call(functools.partial(advect_kernel, tiles, levs, lb, lp, nx,...]
where the time goes in v1:
time: 44.7 us; the launch traced here: 44.5 us
  Pallas kernels  43.8 us (98%)
  between operations  0.64 us (1%)
    pallas_call x1, Pallas kernels, local(): pl.pallas_call(functools.partial(advect_kernel, tiles, levs, lb, lp, nx,...  24.1 us
    pallas_call x1, Pallas kernels, local(): pl.pallas_call(functools.partial(physics_kernel, rows, ny, levels, level_...  19.8 us

profile of v1, /device:TPU:0, one launch (start us, length us, event | category | flops | bytes accessed | tf_op | source)
XLA Modules:
  0.0 44.5 jit_solution(16332940877466634598)
XLA Ops:
  0.6 24.1 %advect.1 = (bf16[32,128,128]{2,1,0:T(8,128)(2,1)}, f32[32,128]{1,0:T(8,128)}, bf16[144,512]{1,0:T(8,128)(2,1)}, bf16[144,512]{1,0:T(8,128)(2,1)}, bf16[288,144]{1,0:T(8,128)(2,1)}) custom-call(f32[3840,128]{1,0:T(8,128)} %bitcast.10, f32[1920,128]{1,0:T(8,128)} %bitcast.11, f32[1920,128]{1,0:T(8,128)} %bitcast.12, f32[1920,128]{1,0:T(8,128)} %bitcast.13, ...), custom_call_target="tpu_custom_call" | custom-call | tf_op jit(solution)/shard_map/advect/pallas_call | solution.py:342
  24.7 19.8 %physics.1 = (f32[60,64,128]{2,1,0:T(8,128)}, f32[8,4096]{1,0:T(8,128)}) custom-call(bf16[32,128,128]{2,1,0:T(8,128)(2,1)} %get-tuple-element.9.feat_ref, f32[8,4096]{1,0:T(8,128)} %surf_ref.1, f32[32,128]{1,0:T(8,128)} %get-tuple-element.10.mask, bf16[144,512]{1,0:T(8,128)(2,1)} %get-tuple-element.11.iw, bf16[5,512,512]{2,1,0:T(8,128)(2,1)} %hw_ref.1, ...), custom_call_target="tpu_custom_call" | custom-call | tf_op jit(solution)/shard_map/physics/pallas_call | solution.py:382

commit v2 on v1

--- a/solution.py
+++ b/solution.py
@@ -16,12 +16,12 @@
 
 
 def advect_kernel(
-    tiles, levs, lb, lp, nx, ny,
+    tiles, levs, lb, lp, nx, ny, levels, level_pad,
     f_hbm, wx_hbm, wy_hbm, d_hbm, *refs,
 ):
-    small_hbm, refs = refs[:7], refs[7:]
-    out_ref, mask, iw, ow, cw = refs[:5]
-    small, refs = refs[5:12], refs[12:]
+    small_hbm, refs = refs[:9], refs[9:]
+    out_ref, mask, iw, ow, cw, fields_ref, surface_ref = refs[:7]
+    small, refs = refs[7:16], refs[16:]
     fv, wv, padded, coef, edge_out, edge_in, outbox, load_sem, small_sem = refs[:9]
     halo_send, halo_recv, part_send, part_recv = refs[9:]
     tile = lax.axis_index("tile")
@@ -177,11 +177,24 @@
 
         section(me * mine + k * ROWS, save)
 
-    @pl.loop(1, steps - 1)
-    def _(k):
-        @pl.loop(pair, levs)
-        def _(o):
-            step(k, o)
+    def batch(first, stride, count):
+        @pl.loop(0, count)
+        def _(i):
+            @pl.loop(pair, levs)
+            def _(o):
+                step(first + i * stride, o)
+
+        @pl.loop(0, count)
+        def _(i):
+            @pl.loop(1, pair)
+            def _(o):
+                step(first + i * stride, o)
+
+        @pl.loop(0, count)
+        def _(i):
+            own(first + i * stride)
+
+    batch(1, 1, steps - 2)
 
     for copy in halos:
         copy.wait()
@@ -189,32 +202,37 @@
         for r in range(2):
             set_coef(first + r, *(edge_in[side, r * 3 + i] for i in range(3)))
 
-    @pl.loop(0, 2)
-    def _(i):
-        @pl.loop(pair, levs)
-        def _(o):
-            step(i * (steps - 1), o)
-
-    @pl.loop(0, steps)
-    def _(k):
-        @pl.loop(1, pair)
-        def _(o):
-            step(k, o)
-
-    @pl.loop(0, steps)
-    def _(k):
-        own(k)
+    batch(0, steps - 1, 2)
 
     for copy in extras:
         copy.wait()
-    prepare(*small, mask, iw, ow, cw)
-
-    @pl.loop(0, steps)
-    def _(k):
+    prepare(*small[:7], mask, iw, ow, cw)
+    hidden, surf_ref = small[7:]
+
+    def finish(k):
         @pl.loop(1, levs)
         def _(o):
             part_copy(k, o, me).wait_send()
             part_copy(k, o, peer(o, -1)).wait_recv()
+
+    flat = fields_ref.reshape(levels * 2 * ROWS * (steps - 2), ny)
+    wide = ROWS * ny
+
+    @pl.loop(1, steps - 1)
+    def _(k):
+        finish(k)
+        at = pl.ds(pl.multiple_of((k - 1) * wide, wide), wide)
+        surface_ref[:, at] = column_physics(
+            [out_ref[k * ROWS + r] for r in range(ROWS)],
+            [mask[pl.ds(k * ROWS + r, 1), :] for r in range(ROWS)],
+            surf_ref[:, pl.ds(pl.multiple_of(k * wide, wide), wide)],
+            iw, hidden, ow, cw, levels, level_pad,
+            flat, 2 * ROWS * (k - 1), 2 * ROWS * (steps - 2),
+        )
+
+    @pl.loop(0, 2)
+    def _(i):
+        finish(i * (steps - 1))
 
 
 def nt(a, b):
@@ -243,25 +261,23 @@
     return h * jnp.tanh(h) + h
 
 
-def physics_kernel(
-    rows, lanes, levels, level_pad, layers,
-    feat_ref, surf_ref, mask, iw, hw_ref, ow, cw, fields_ref, surface_ref,
+def column_physics(
+    feat, masks, surf, iw, hidden, ow, cw, levels, level_pad, flat, place, stride
 ):
-    step = pl.program_id(0)
-    surf = surf_ref[...]
+    rows, lanes = len(feat), feat[0].shape[1]
     surf16 = surf.astype(BF16)
     tail = jnp.concatenate([surf16, jnp.zeros_like(surf16)], axis=0)
-    feat = jnp.concatenate([feat_ref[r] for r in range(rows)], axis=1)
-    feat = jnp.concatenate([feat, tail], axis=0)
-
-    half = rows * lanes // 2
+    feat = jnp.concatenate([jnp.concatenate(feat, axis=1), tail], axis=0)
+
+    per = rows // 2
+    half = per * lanes
     streams = []
     for s in range(2):
         piece = feat[:, s * half : (s + 1) * half]
         streams.append(
             silu(lax.dot_general(piece, iw[...], (((0,), (0,)), ((), ())), preferred_element_type=F32))
         )
-    hid = hw_ref.shape[2]
+    layers, _, hid = hidden.shape
     cuts = [slice(c, min(c + 256, hid)) for c in range(0, hid, 256)]
     for layer in range(layers):
         for s in range(2):
@@ -269,19 +285,17 @@
             streams[s] = jnp.concatenate(
                 [
                     streams[s][:, cut]
-                    + silu(jnp.dot(operand, hw_ref[layer, :, cut], preferred_element_type=F32))
+                    + silu(jnp.dot(operand, hidden[layer, :, cut], preferred_element_type=F32))
                     for cut in cuts
                 ],
                 axis=1,
             )
     both = jnp.dot(cw[...], feat, preferred_element_type=F32)
     out_rows = ow.shape[0]
-    flat = fields_ref.reshape(levels * 2 * rows, lanes)
+    surfaces = []
     for s in range(2):
         physics = nt(ow[...], streams[s].astype(BF16)).astype(BF16).astype(F32)
-        keep = jnp.concatenate(
-            [mask[pl.ds(step * rows + s * (rows // 2) + r, 1), :] for r in range(rows // 2)], axis=1
-        )
+        keep = jnp.concatenate(masks[s * per : (s + 1) * per], axis=1)
         at = slice(s * half, (s + 1) * half)
         tend = both[:out_rows, at] + jnp.where(keep > 0.5, physics, 0.0)
         tend = tend.astype(BF16).astype(F32)
@@ -291,14 +305,38 @@
                 both[out_rows + first : out_rows + first + level_pad, at]
                 + tend[first : first + level_pad]
             )
-            for r in range(rows // 2):
-                place = 2 * (s * (rows // 2) + r) + v
+            for r in range(per):
                 for l in range(0, levels, 8):
                     n = min(8, levels - l)
-                    flat[pl.ds(l * 2 * rows + place, n, stride=2 * rows), :] = (
+                    start = l * stride + place + 2 * (s * per + r) + v
+                    flat[pl.ds(start, n, stride=stride), :] = (
                         total[l : l + n, r * lanes : (r + 1) * lanes]
                     )
-        surface_ref[:, at] = surf[:, at] + tend[2 * level_pad : 2 * level_pad + surf.shape[0]]
+        surfaces.append(surf[:, at] + tend[2 * level_pad : 2 * level_pad + surf.shape[0]])
+    return jnp.concatenate(surfaces, axis=1)
+
+
+def physics_kernel(
+    steps, lanes, levels, level_pad,
+    feat_ref, surf_ref, part_ref, surf_part_ref, mask, iw, hidden, ow, cw,
+    fields_ref, surface_ref,
+):
+    step = pl.program_id(0)
+    inner = jnp.logical_and(step > 0, step < steps - 1)
+
+    @pl.when(inner)
+    def _():
+        fields_ref[...] = part_ref[...]
+        surface_ref[...] = surf_part_ref[...]
+
+    @pl.when(jnp.logical_not(inner))
+    def _():
+        flat = fields_ref.reshape(levels * 2 * ROWS, lanes)
+        surface_ref[...] = column_physics(
+            [feat_ref[r] for r in range(ROWS)],
+            [mask[pl.ds(step * ROWS + r, 1), :] for r in range(ROWS)],
+            surf_ref[...], iw, hidden, ow, cw, levels, level_pad, flat, 0, 2 * ROWS,
+        )
 
 
 def orders(levs, lb, lp, levels, level_pad, surf, features):
@@ -333,23 +371,25 @@
     parts = mine // ROWS
     surf, cols = surface.shape
     features, hid = input_weight.shape
-    layers = hidden_weight.shape[0]
     orderings = [
         jnp.asarray(m, BF16) for m in orders(levs, lb, lp, levels, level_pad, surf, features)
     ]
     size_out, size_in = orderings[2].shape
     small = [cloud_list.reshape(1, -1), *orderings, input_weight, output_weight, clear_weight]
-    feats, mask, iw, ow, cw = pl.pallas_call(
-        functools.partial(advect_kernel, tiles, levs, lb, lp, nx, ny),
+    small += [hidden_weight, surface]
+    feats, mask, iw, ow, cw, part, surf_part = pl.pallas_call(
+        functools.partial(advect_kernel, tiles, levs, lb, lp, nx, ny, levels, level_pad),
         out_shape=(
             jax.ShapeDtypeStruct((mine, levs * group, ny), BF16),
             jax.ShapeDtypeStruct((mine, ny), F32),
             jax.ShapeDtypeStruct((size_in, hid), BF16),
             jax.ShapeDtypeStruct((size_out, hid), BF16),
             jax.ShapeDtypeStruct((2 * size_out, size_in), BF16),
+            jax.ShapeDtypeStruct((levels, 2 * ROWS * (parts - 2), ny), F32),
+            jax.ShapeDtypeStruct((surf, ROWS * (parts - 2) * ny), F32),
         ),
         in_specs=[any_spec] * (4 + len(small)),
-        out_specs=(vmem_spec,) * 5,
+        out_specs=(vmem_spec,) * 7,
         scratch_shapes=[pltpu.VMEM(a.shape, a.dtype) for a in small] + [
             pltpu.VMEM(((2 * lb + lp - lb) * nx, ny), F32),
             pltpu.VMEM((3 * lp * nx, ny), F32),
@@ -377,26 +417,31 @@
         *small,
     )
 
-    rows = 8
-    wide = rows * ny
+    wide = ROWS * ny
+
+    def inner(i):
+        return jnp.clip(i - 1, 0, parts - 3)
+
     fields_out, surface_out = pl.pallas_call(
-        functools.partial(physics_kernel, rows, ny, levels, level_pad, layers),
-        grid=(mine // rows,),
+        functools.partial(physics_kernel, parts, ny, levels, level_pad),
+        grid=(parts,),
         out_shape=(
             jax.ShapeDtypeStruct((levels, mine * 2, ny), F32),
             jax.ShapeDtypeStruct((surf, cols), F32),
         ),
         in_specs=[
-            pl.BlockSpec((rows, levs * group, ny), lambda i: (i, 0, 0)),
+            pl.BlockSpec((ROWS, levs * group, ny), lambda i: (i, 0, 0)),
             pl.BlockSpec((surf, wide), lambda i: (0, i)),
+            pl.BlockSpec((levels, 2 * ROWS, ny), lambda i: (0, inner(i), 0)),
+            pl.BlockSpec((surf, wide), lambda i: (0, inner(i))),
         ] + [vmem_spec] * 5,
         out_specs=(
-            pl.BlockSpec((levels, 2 * rows, ny), lambda i: (0, i, 0)),
+            pl.BlockSpec((levels, 2 * ROWS, ny), lambda i: (0, i, 0)),
             pl.BlockSpec((surf, wide), lambda i: (0, i)),
         ),
         compiler_params=pltpu.CompilerParams(vmem_limit_bytes=PHYSICS_VMEM),
         name="physics",
-    )(feats, surface, mask, iw, hidden_weight, ow, cw)
+    )(feats, surface, part, surf_part, mask, iw, hidden_weight, ow, cw)
     fields_out = fields_out.reshape(levels, mine, 2, ny).transpose(2, 0, 1, 3)
     return fields_out.reshape(2, levels, cols), surface_out
 

time: 44.7 us -> 42.5 us (0.951)
  Pallas kernels: 43.8 us -> 41.7 us
    pallas_call x1, Pallas kernels: 19.8 us -> 13.1 us  [local(): pl.pallas_call(functools.partial(physics_kernel, parts, ny, levels, level...]
    pallas_call x1, Pallas kernels: 24.1 us -> 28.6 us  [local(): pl.pallas_call(functools.partial(advect_kernel, tiles, levs, lb, lp, nx,...]
where the time goes in v2:
time: 42.5 us; the launch traced here: 42.3 us
  Pallas kernels  41.7 us (98%)
  between operations  0.64 us (2%)
    pallas_call x1, Pallas kernels, local(): pl.pallas_call(functools.partial(advect_kernel, tiles, levs, lb, lp, nx,...  28.6 us
    pallas_call x1, Pallas kernels, local(): pl.pallas_call(functools.partial(physics_kernel, parts, ny, levels, level...  13.1 us

profile of v2, /device:TPU:0, one launch (start us, length us, event | category | flops | bytes accessed | tf_op | source)
XLA Modules:
  0.0 42.3 jit_solution(7118506912280835391)
XLA Ops:
  0.6 28.6 %advect.1 = (bf16[32,128,128]{2,1,0:T(8,128)(2,1)}, f32[32,128]{1,0:T(8,128)}, bf16[144,512]{1,0:T(8,128)(2,1)}, bf16[144,512]{1,0:T(8,128)(2,1)}, bf16[288,144]...) custom-call(f32[3840,128]{1,0:T(8,128)} %bitcast.10, f32[1920,128]{1,0:T(8,128)} %bitcast.11, ...), custom_call_target="tpu_custom_call" | custom-call | tf_op jit(solution)/shard_map/advect/pallas_call | solution.py:380
  29.2 13.1 %physics.1 = (f32[60,64,128]{2,1,0:T(8,128)}, f32[8,4096]{1,0:T(8,128)}) custom-call(bf16[32,128,128]{2,1,0:T(8,128)(2,1)} %get-tuple-element.11.feat_ref, f32[8,4096]{1,0:T(8,128)} %surf_ref.1, f32[60,32,128]{2,1,0:T(8,128)} %get-tuple-element.12.part_ref, f32[8,2048]{1,0:T(8,128)} %get-tuple-element.13.surf_part_ref, f32[32,128]{1,0:T(8,128)} %get-tuple-element.14.mask, ...), custom_call_target="tpu_custom_call" | custom-call | tf_op jit(solution)/shard_map/physics/pallas_call | solution.py:425

commit v3 on v2

--- a/solution.py
+++ b/solution.py
@@ -12,7 +12,6 @@
 BF16 = jnp.bfloat16
 ROWS = 8
 ADVECT_VMEM = 58 * 1024 * 1024
-PHYSICS_VMEM = 58 * 1024 * 1024
 
 
 def advect_kernel(
@@ -20,8 +19,9 @@
     f_hbm, wx_hbm, wy_hbm, d_hbm, *refs,
 ):
     small_hbm, refs = refs[:9], refs[9:]
-    out_ref, mask, iw, ow, cw, fields_ref, surface_ref = refs[:7]
-    small, refs = refs[7:16], refs[16:]
+    fields_hbm, surface_ref = refs[:2]
+    out_ref, mask, iw, ow, cw, flat, out_sem = refs[2:9]
+    small, refs = refs[9:18], refs[18:]
     fv, wv, padded, coef, edge_out, edge_in, outbox, load_sem, small_sem = refs[:9]
     halo_send, halo_recv, part_send, part_recv = refs[9:]
     tile = lax.axis_index("tile")
@@ -119,30 +119,36 @@
         for r in range(2):
             convert(3 + b * 2 + r)
 
-    def rate(c, e, w, row):
+    def rate(c, e, w, weights):
         north = pltpu.roll(c, ny - 1, axis=1)
         south = pltpu.roll(c, 1, axis=1)
         return (
-            coef[row, 0] * e + coef[row, 1] * w + coef[row, 2] * north + coef[row, 3] * south
-            - coef[row, 4] * c
+            weights[0] * e + weights[1] * w + weights[2] * north + weights[3] * south
+            - weights[4] * c
         )
 
     def section(x0, save):
-        for v in range(2):
-            lo, hi = v * lp, (v + 1) * lp
-            f = [padded[x0 + i, lo:hi, :] for i in range(2)]
-            one = []
-            two = []
-            for r in range(ROWS + 4):
-                f.append(padded[x0 + r + 2, lo:hi, :])
-                one.append(f[r + 1] + rate(f[r + 1], f[r + 2], f[r], x0 + r) * (1.0 / 3.0))
-                if r >= 2:
-                    two.append(
-                        f[r] + 0.5 * rate(one[r - 1], one[r], one[r - 2], x0 + r - 1)
-                    )
-                if r >= 4:
-                    done = f[r - 1] + rate(two[r - 3], two[r - 2], two[r - 4], x0 + r - 2)
-                    save(r - 4, lo, done.astype(BF16))
+        cuts = [slice(v * lp, (v + 1) * lp) for v in range(2)]
+        f = [[padded[x0 + i, cut, :] for i in range(2)] for cut in cuts]
+        one = [[], []]
+        two = [[], []]
+        for r in range(ROWS + 4):
+            weights = [coef[x0 + r, i] for i in range(5)]
+            for v in range(2):
+                g = f[v]
+                g.append(padded[x0 + r + 2, cuts[v], :])
+                one[v].append(g[r + 1] + rate(g[r + 1], g[r + 2], g[r], weights) * (1.0 / 3.0))
+            if r >= 2:
+                weights = [coef[x0 + r - 1, i] for i in range(5)]
+                for v in range(2):
+                    o = one[v]
+                    two[v].append(f[v][r] + 0.5 * rate(o[r - 1], o[r], o[r - 2], weights))
+            if r >= 4:
+                weights = [coef[x0 + r - 2, i] for i in range(5)]
+                for v in range(2):
+                    t = two[v]
+                    done = f[v][r - 1] + rate(t[r - 3], t[r - 2], t[r - 4], weights)
+                    save(r - 4, v * lp, done.astype(BF16))
 
     pair = 2 if levs % 2 == 0 else 1
     chips = levs // pair
@@ -215,24 +221,33 @@
             part_copy(k, o, me).wait_send()
             part_copy(k, o, peer(o, -1)).wait_recv()
 
-    flat = fields_ref.reshape(levels * 2 * ROWS * (steps - 2), ny)
     wide = ROWS * ny
-
-    @pl.loop(1, steps - 1)
-    def _(k):
+    blocks = flat.reshape(levels, 2 * mine, ny)
+
+    def write(k):
+        at = pl.ds(pl.multiple_of(k * 2 * ROWS, 2 * ROWS), 2 * ROWS)
+        return pltpu.make_async_copy(
+            blocks.at[:, at, :], fields_hbm.at[:, at, :], out_sem.at[k]
+        )
+
+    def columns(k):
         finish(k)
-        at = pl.ds(pl.multiple_of((k - 1) * wide, wide), wide)
+        at = pl.ds(pl.multiple_of(k * wide, wide), wide)
         surface_ref[:, at] = column_physics(
             [out_ref[k * ROWS + r] for r in range(ROWS)],
             [mask[pl.ds(k * ROWS + r, 1), :] for r in range(ROWS)],
-            surf_ref[:, pl.ds(pl.multiple_of(k * wide, wide), wide)],
-            iw, hidden, ow, cw, levels, level_pad,
-            flat, 2 * ROWS * (k - 1), 2 * ROWS * (steps - 2),
-        )
-
-    @pl.loop(0, 2)
+            surf_ref[:, at], iw, hidden, ow, cw, levels, level_pad,
+            flat, 2 * ROWS * k, 2 * mine,
+        )
+        write(k).start()
+
+    @pl.loop(0, steps)
     def _(i):
-        finish(i * (steps - 1))
+        columns(lax.rem(i + 1, steps - 1) + (i // (steps - 1)) * (steps - 2))
+
+    @pl.loop(0, steps)
+    def _(k):
+        write(k).wait()
 
 
 def nt(a, b):
@@ -316,29 +331,6 @@
     return jnp.concatenate(surfaces, axis=1)
 
 
-def physics_kernel(
-    steps, lanes, levels, level_pad,
-    feat_ref, surf_ref, part_ref, surf_part_ref, mask, iw, hidden, ow, cw,
-    fields_ref, surface_ref,
-):
-    step = pl.program_id(0)
-    inner = jnp.logical_and(step > 0, step < steps - 1)
-
-    @pl.when(inner)
-    def _():
-        fields_ref[...] = part_ref[...]
-        surface_ref[...] = surf_part_ref[...]
-
-    @pl.when(jnp.logical_not(inner))
-    def _():
-        flat = fields_ref.reshape(levels * 2 * ROWS, lanes)
-        surface_ref[...] = column_physics(
-            [feat_ref[r] for r in range(ROWS)],
-            [mask[pl.ds(step * ROWS + r, 1), :] for r in range(ROWS)],
-            surf_ref[...], iw, hidden, ow, cw, levels, level_pad, flat, 0, 2 * ROWS,
-        )
-
-
 def orders(levs, lb, lp, levels, level_pad, surf, features):
     size_in = levs * 2 * lp + 2 * surf
     size_out = 2 * level_pad + 2 * surf
@@ -377,20 +369,23 @@
     size_out, size_in = orderings[2].shape
     small = [cloud_list.reshape(1, -1), *orderings, input_weight, output_weight, clear_weight]
     small += [hidden_weight, surface]
-    feats, mask, iw, ow, cw, part, surf_part = pl.pallas_call(
+    fields_out, surface_out = pl.pallas_call(
         functools.partial(advect_kernel, tiles, levs, lb, lp, nx, ny, levels, level_pad),
         out_shape=(
-            jax.ShapeDtypeStruct((mine, levs * group, ny), BF16),
-            jax.ShapeDtypeStruct((mine, ny), F32),
-            jax.ShapeDtypeStruct((size_in, hid), BF16),
-            jax.ShapeDtypeStruct((size_out, hid), BF16),
-            jax.ShapeDtypeStruct((2 * size_out, size_in), BF16),
-            jax.ShapeDtypeStruct((levels, 2 * ROWS * (parts - 2), ny), F32),
-            jax.ShapeDtypeStruct((surf, ROWS * (parts - 2) * ny), F32),
+            jax.ShapeDtypeStruct((levels, mine * 2, ny), F32),
+            jax.ShapeDtypeStruct((surf, cols), F32),
         ),
         in_specs=[any_spec] * (4 + len(small)),
-        out_specs=(vmem_spec,) * 7,
-        scratch_shapes=[pltpu.VMEM(a.shape, a.dtype) for a in small] + [
+        out_specs=(any_spec, vmem_spec),
+        scratch_shapes=[
+            pltpu.VMEM((mine, levs * group, ny), BF16),
+            pltpu.VMEM((mine, ny), F32),
+            pltpu.VMEM((size_in, hid), BF16),
+            pltpu.VMEM((size_out, hid), BF16),
+            pltpu.VMEM((2 * size_out, size_in), BF16),
+            pltpu.VMEM((levels * mine * 2, ny), F32),
+            pltpu.SemaphoreType.DMA((parts,)),
+        ] + [pltpu.VMEM(a.shape, a.dtype) for a in small] + [
             pltpu.VMEM(((2 * lb + lp - lb) * nx, ny), F32),
             pltpu.VMEM((3 * lp * nx, ny), F32),
             pltpu.VMEM((nx + 6, group, ny), F32),
@@ -417,31 +412,6 @@
         *small,
     )
 
-    wide = ROWS * ny
-
-    def inner(i):
-        return jnp.clip(i - 1, 0, parts - 3)
-
-    fields_out, surface_out = pl.pallas_call(
-        functools.partial(physics_kernel, parts, ny, levels, level_pad),
-        grid=(parts,),
-        out_shape=(
-            jax.ShapeDtypeStruct((levels, mine * 2, ny), F32),
-            jax.ShapeDtypeStruct((surf, cols), F32),
-        ),
-        in_specs=[
-            pl.BlockSpec((ROWS, levs * group, ny), lambda i: (i, 0, 0)),
-            pl.BlockSpec((surf, wide), lambda i: (0, i)),
-            pl.BlockSpec((levels, 2 * ROWS, ny), lambda i: (0, inner(i), 0)),
-            pl.BlockSpec((surf, wide), lambda i: (0, inner(i))),
-        ] + [vmem_spec] * 5,
-        out_specs=(
-            pl.BlockSpec((levels, 2 * ROWS, ny), lambda i: (0, i, 0)),
-            pl.BlockSpec((surf, wide), lambda i: (0, i)),
-        ),
-        compiler_params=pltpu.CompilerParams(vmem_limit_bytes=PHYSICS_VMEM),
-        name="physics",
-    )(feats, surface, part, surf_part, mask, iw, hidden_weight, ow, cw)
     fields_out = fields_out.reshape(levels, mine, 2, ny).transpose(2, 0, 1, 3)
     return fields_out.reshape(2, levels, cols), surface_out
 

time: 42.5 us -> 41.2 us (0.969)
  Pallas kernels: 41.7 us -> 36.7 us
  local copies, waits for them, and re-layouts: 0 us -> 3.74 us
    pallas_call x1 -> x0, Pallas kernels: 13.1 us -> none  [local(): pl.pallas_call(functools.partial(physics_kernel, parts, ny, levels, level...]
    pallas_call x1, Pallas kernels: 28.6 us -> 36.7 us  [local(): pl.pallas_call(functools.partial(advect_kernel, tiles, levs, lb, lp, nx,...]
    unnamed x0 -> x4, local copies, waits for them, and re-layouts: none -> 3.74 us
where the time goes in v3:
time: 41.2 us; the launch traced here: 41.1 us
  Pallas kernels  36.7 us (89%)
  local copies, waits for them, and re-layouts  3.74 us (9%)
  between operations  0.65 us (2%)
    pallas_call x1, Pallas kernels, local(): pl.pallas_call(functools.partial(advect_kernel, tiles, levs, lb, lp, nx,...  36.7 us
    unnamed x4, local copies, waits for them, and re-layouts  3.74 us

profile of v3, /device:TPU:0, one launch (start us, length us, event | category | flops | bytes accessed | tf_op | source)
XLA Modules:
  0.0 41.1 jit_solution(12216056625955000103)
XLA Ops:
  0.6 36.7 %advect.1 = (f32[60,64,128]{2,1,0:T(8,128)}, f32[8,4096]{1,0:T(8,128)}) custom-call(f32[3840,128]{1,0:T(8,128)} %bitcast.11, f32[1920,128]{1,0:T(8,128)} %bitcast.12, f32[1920,128]{1,0:T(8,128)} %bitcast.13, f32[1920,128]{1,0:T(8,128)} %bitcast.14, s32[1,4096]{1,0:T(1,128)} %bitcast.15, bf16[144,128]{1,0:T(8,128)(2,1)} %constant.6.clone.refs_1_, ...), custom_call_target="tpu_custom_call" | custom-call | tf_op jit(solution)/shard_map/advect/pallas_call | solution.py:372
  37.3 0.0 copy-start
  37.3 3.1 %copy.18 = f32[2,60,4096]{2,0,1:T(2,128)} copy(f32[2,60,4096]{2,0,1:T(2,128)} %bitcast.10) | data formatting | bytes 3932160
  40.4 0.0 copy-done
  40.4 0.7 %copy.19 = f32[8,4096]{1,0:T(8,128)} copy(f32[8,4096]{1,0:T(8,128)S(1)} %copy-done) | data formatting | bytes 262144
Async XLA Ops:
  37.3 3.1 %copy-start = (f32[8,4096]{1,0:T(8,128)S(1)}, f32[8,4096]{1,0:T(8,128)}, u32[]{:S(2)}) copy-start(f32[8,4096]{1,0:T(8,128)} %get-tuple-element.9) | copy-start | bytes 393220
